TPU v7x, 32 devices: a whole 2x2x4 slice. The times are simulated.
32 devices in a mesh: space: 8 (over z, x), kern: 4 (over y, core).
Axes of the slice: x: 2, y: 2, z: 4, core: 2. Of those that a mesh axis runs over, the one named last changes fastest.
Arguments:
- mask: bfloat16 [4096, 4096], P('space'), may hold values from -1 to 1
- kernels: float32 [2, 16, 512, 512], P(None, 'kern', 'space'), may hold values from -4 to 4
- target: int32 [1024, 1024], P('space'), may hold values 0 or 1
Outputs:
- gradient: float32 [4096, 4096], P('space')
- resist: float32 [1024, 1024], P('space')
All inputs are finite; a program needn't handle non-finite values. No bound on the sum of `target` on one device may be relied on, other than what follows from the above.
Results may differ from a plain program's by a relative error of at most 0.0003.
Values sent between devices are 32-bit elements; how exact they have to be, the bound alone decides.
A program may use at most 64 MiB of HBM per device.

v0:
```python
import jax
import jax.numpy as jnp
from jax import lax
from jax.sharding import PartitionSpec as P

N = 4096
B = 512
G = 1024


steepness = 8.0
threshold = 1.5
highest = lax.Precision.HIGHEST
block_limit = 1024


def phases(left, right, modulus):
    product = left[:, None] * right[None, :] % modulus
    return product.astype(jnp.float32) * (2.0 * jnp.pi / modulus)


def column_table(pixels, frequency, length):
    angle = phases(pixels, frequency, length)
    return jnp.concatenate([jnp.cos(angle), -jnp.sin(angle)], axis=1)


def row_table(pixels, frequency, length):
    angle = phases(pixels, frequency, length)
    return jnp.concatenate([jnp.cos(angle), -jnp.sin(angle)], axis=1) / length


def grid_table(frequency, points):
    angle = phases(frequency, jnp.arange(points, dtype=jnp.int32), points)
    return jnp.concatenate([jnp.cos(angle), jnp.sin(angle)], axis=1)


def forward_columns(mask, frequency):
    rows = mask.shape[0]
    span = min(block_limit, N)
    count = frequency.shape[0]

    def step(index, running):
        start = index * span
        table = column_table(start + jnp.arange(span, dtype=jnp.int32), frequency, N)
        piece = lax.dynamic_slice_in_dim(mask, start, span, 1).astype(jnp.float32)
        return running + lax.dot_general(table, piece, (((0,), (1,)), ((), ())), precision=highest)

    running = lax.fori_loop(0, N // span, step, jnp.zeros((2 * count, rows), jnp.float32))
    return running.reshape(2, count, rows)


def forward_rows(arrived):
    count = arrived.shape[1]
    flat = arrived.reshape(2 * count, N)
    frequency = jnp.arange(B, dtype=jnp.int32) - B // 2
    span = min(block_limit, N)

    def step(index, running):
        start = index * span
        table = row_table(start + jnp.arange(span, dtype=jnp.int32), frequency, N)
        piece = lax.dynamic_slice_in_dim(flat, start, span, 1)
        return running + jnp.dot(piece, table, precision=highest)

    running = lax.fori_loop(0, N // span, step, jnp.zeros((2 * count, 2 * B), jnp.float32))
    real_part = running[:count, :B] - running[count:, B:]
    imag_part = running[:count, B:] + running[count:, :B]
    return jnp.stack([real_part, imag_part])


def adjoint_rows(sum_re, sum_im):
    count = sum_re.shape[0]
    stacked = jnp.concatenate(
        [jnp.concatenate([sum_re, sum_im], axis=1), jnp.concatenate([sum_im, -sum_re], axis=1)],
        axis=0,
    )
    frequency = jnp.arange(B, dtype=jnp.int32) - B // 2
    span = min(block_limit, N)

    def step(index, output):
        start = index * span
        table = row_table(start + jnp.arange(span, dtype=jnp.int32), frequency, N)
        piece = lax.dot_general(stacked, table, (((1,), (1,)), ((), ())), precision=highest)
        return lax.dynamic_update_slice_in_dim(output, piece, start, 1)

    output = lax.fori_loop(0, N // span, step, jnp.zeros((2 * count, N), jnp.float32))
    return output.reshape(2, count, N)


def add_columns(total, spectrum, frequency):
    span = min(block_limit, N)

    def step(index, running):
        start = index * span
        table = column_table(start + jnp.arange(span, dtype=jnp.int32), frequency, N)
        piece = lax.dot_general(spectrum, table, (((0,), (1,)), ((), ())), precision=highest)
        current = lax.dynamic_slice_in_dim(running, start, span, 1)
        return lax.dynamic_update_slice_in_dim(running, current + piece, start, 1)

    return lax.fori_loop(0, N // span, step, total)


def local(mask, kernels, target):
    rows = mask.shape[0]
    kern_count = lax.axis_size("kern")
    space_count = lax.axis_size("space")
    group = lax.axis_index("kern")
    per_space = B // space_count
    per_group = per_space // kern_count
    frequency = jnp.arange(B, dtype=jnp.int32) - B // 2
    subset = (
        per_space * jnp.arange(space_count, dtype=jnp.int32)[:, None]
        + per_group * group
        + jnp.arange(per_group, dtype=jnp.int32)[None, :]
    )
    columns = forward_columns(mask, subset.reshape(-1) - B // 2)
    arrived = lax.all_to_all(columns, "space", split_axis=1, concat_axis=2, tiled=True)
    spectrum = lax.all_gather(forward_rows(arrived), "kern", axis=1, tiled=True)
    kern_swap = jnp.swapaxes(kernels, 1, 2)
    kernel_count = kern_swap.shape[2]
    spec_re = spectrum[0][:, None, :]
    spec_im = spectrum[1][:, None, :]
    prod_re = kern_swap[0] * spec_re - kern_swap[1] * spec_im
    prod_im = kern_swap[0] * spec_im + kern_swap[1] * spec_re
    grid = grid_table(frequency, G)
    lifted = jnp.dot(
        jnp.stack([prod_re, prod_im]).reshape(2 * per_space * kernel_count, B),
        grid,
        precision=highest,
    )
    lifted = lifted.reshape(2, per_space, kernel_count, 2 * G)
    coarse_re = lifted[0, :, :, :G] - lifted[1, :, :, G:]
    coarse_im = lifted[0, :, :, G:] + lifted[1, :, :, :G]
    coarse = jnp.stack([coarse_re, coarse_im], axis=1)
    gathered = lax.all_to_all(coarse, "space", split_axis=3, concat_axis=0, tiled=True)
    grid_rows = gathered.shape[3]
    image = lax.dot_general(
        gathered.reshape(B, 2 * kernel_count * grid_rows),
        grid,
        (((0,), (0,)), ((), ())),
        precision=highest,
    )
    image = image.reshape(2, kernel_count, grid_rows, 2 * G)
    field_re = image[0, :, :, :G] - image[1, :, :, G:]
    field_im = image[0, :, :, G:] + image[1, :, :, :G]
    partial_light = jnp.sum(field_re * field_re + field_im * field_im, axis=0) / (B * B)
    intensity = lax.psum(partial_light, "kern")
    resist = jax.nn.sigmoid(steepness * (intensity - threshold))
    slope = 2.0 * (resist - target.astype(jnp.float32)) * steepness * resist * (1.0 - resist)
    scale = 2.0 * slope / (B * B)
    grad_re = scale * field_re
    grad_im = scale * field_im
    mixed = jnp.stack(
        [
            jnp.concatenate([grad_re, grad_im], axis=-1),
            jnp.concatenate([grad_im, -grad_re], axis=-1),
        ]
    )
    mixed = mixed.reshape(2 * kernel_count * grid_rows, 2 * G)
    backward = lax.dot_general(grid, mixed, (((1,), (1,)), ((), ())), precision=highest)
    backward = backward.reshape(B, 2, kernel_count, grid_rows)
    returned = lax.all_to_all(backward, "space", split_axis=0, concat_axis=3, tiled=True)
    back_re = returned[:, 0]
    back_im = returned[:, 1]
    mixed_two = jnp.stack(
        [
            jnp.concatenate([back_re, back_im], axis=-1),
            jnp.concatenate([back_im, -back_re], axis=-1),
        ]
    )
    mixed_two = mixed_two.reshape(2 * per_space * kernel_count, 2 * G)
    spectral = lax.dot_general(mixed_two, grid, (((1,), (1,)), ((), ())), precision=highest)
    spectral = spectral.reshape(2, per_space, kernel_count, B)
    sum_re = jnp.sum(kern_swap[0] * spectral[0] + kern_swap[1] * spectral[1], axis=1)
    sum_im = jnp.sum(kern_swap[0] * spectral[1] - kern_swap[1] * spectral[0], axis=1)
    empty = jnp.zeros((rows, N), jnp.float32)
    shares = (
        lax.psum_scatter(sum_re, "kern", scatter_dimension=0, tiled=True),
        lax.psum_scatter(sum_im, "kern", scatter_dimension=0, tiled=True),
    )
    delta = adjoint_rows(shares[0], shares[1])
    landed = lax.all_to_all(delta, "space", split_axis=2, concat_axis=1, tiled=True)
    ordering = (
        per_group * jnp.arange(kern_count, dtype=jnp.int32)[:, None, None]
        + per_space * jnp.arange(space_count, dtype=jnp.int32)[None, :, None]
        + jnp.arange(per_group, dtype=jnp.int32)[None, None, :]
    )
    ordered_freq = ordering.reshape(-1) - B // 2
    piece = lax.all_gather(landed, "kern", axis=1, tiled=True)
    width = piece.shape[1]
    gradient = add_columns(empty, piece.reshape(2 * width, rows), ordered_freq)
    return (gradient, resist)


def solution(mesh):
    in_specs = (P("space", None), P(None, "kern", "space", None), P("space", None))
    out_specs = (P("space", None), P("space", None))
    return jax.shard_map(local, mesh=mesh, in_specs=in_specs, out_specs=out_specs, check_vma=False)
```

profile of v0, /device:TPU:0, one launch (start us, length us, event | category | flops | bytes accessed | tf_op | source)
XLA Modules:
  0.0 641.8 jit_solution(11022036640361063977)
XLA Ops:
  7.2 22.0 %while.66 = (s32[]{:T(128)}, f32[256,512]{1,0:T(8,128)S(1)}, bf16[512,4096]{1,0:T(8,128)(2,1)}, s32[8]{0:T(128)S(1)}, s32[]{:T(128)}, /*index=5*/s32[]{:T(128)}, s32[]{:T(128)}, s32[]{:T(128)}) while((s32[]{:T(128)}, f32[256,512]{1,0:T(8,128)S(1)}, bf16[512,4096]{1,0:T(8,128)(2,1)}, s32[8]{0:T(128)S(1)}, s32[]{:T(128)}, ...), condition=%wide.region_1.2_spmd.clone, body=%wide.region_0.1_spmd.clone.sunk | while | flops 1613104384 | bytes 4204733 | solution.py:48
  37.7 9.6 %fusion.78 = (f32[512,1024]{1,0:T(8,128)S(1)}, f32[512,1024]{1,0:T(8,128)}) fusion(s32[512]{0:T(512)S(1)} %iota_add_fusion.6), kind=kLoop, calls=%fused_computation.130 | loop fusion | flops 7340032 | bytes 4196352 | tf_op jit(solution)/shard_map/cos | solution.py:34
  53.6 47.6 %while.67 = (s32[]{:T(128)}, f32[32,1024]{1,0:T(8,128)S(1)}, f32[32,4096]{1,0:T(8,128)}, s32[]{:T(128)}, s32[]{:T(128)}, /*index=5*/s32[]{:T(128)}, s32[]{:T(128)}) while((s32[]{:T(128)}, f32[32,1024]{1,0:T(8,128)S(1)}, f32[32,4096]{1,0:T(8,128)}, s32[]{:T(128)}, s32[]{:T(128)}, /*index=5*/s32[]{:T(128)}, s32[]{:T(128)}) %tuple.199), condition=%wide.region_3.4_spmd.clone, body=%wide.region_2.3_spmd.clone.sunk | while | flops 412681728 | bytes 8794261 | solution.py:64
  53.9 8.3 %fusion.116 = (f32[1024,512]{1,0:T(8,128)S(1)}, f32[1024,512]{1,0:T(8,128)S(1)}) fusion(s32[512]{0:T(512)S(1)} %iota_add_fusion.17, s32[1024]{0:T(1024)S(1)} %iota_add_fusion.18), kind=kLoop, calls=%fused_computation.79.clone.1 | loop fusion | flops 7864320 | bytes 4200448 | tf_op jit(solution)/shard_map/while/body/eval_jaxpr/cos | solution.py:29
  65.7 8.3 %fusion.116 = (f32[1024,512]{1,0:T(8,128)S(1)}, f32[1024,512]{1,0:T(8,128)S(1)}) fusion(s32[512]{0:T(512)S(1)} %iota_add_fusion.17, s32[1024]{0:T(1024)S(1)} %iota_add_fusion.18), kind=kLoop, calls=%fused_computation.79.clone.1 | loop fusion | flops 7864320 | bytes 4200448 | tf_op jit(solution)/shard_map/while/body/eval_jaxpr/cos | solution.py:29
  77.6 8.3 %fusion.116 = (f32[1024,512]{1,0:T(8,128)S(1)}, f32[1024,512]{1,0:T(8,128)S(1)}) fusion(s32[512]{0:T(512)S(1)} %iota_add_fusion.17, s32[1024]{0:T(1024)S(1)} %iota_add_fusion.18), kind=kLoop, calls=%fused_computation.79.clone.1 | loop fusion | flops 7864320 | bytes 4200448 | tf_op jit(solution)/shard_map/while/body/eval_jaxpr/cos | solution.py:29
  89.4 8.3 %fusion.116 = (f32[1024,512]{1,0:T(8,128)S(1)}, f32[1024,512]{1,0:T(8,128)S(1)}) fusion(s32[512]{0:T(512)S(1)} %iota_add_fusion.17, s32[1024]{0:T(1024)S(1)} %iota_add_fusion.18), kind=kLoop, calls=%fused_computation.79.clone.1 | loop fusion | flops 7864320 | bytes 4200448 | tf_op jit(solution)/shard_map/while/body/eval_jaxpr/cos | solution.py:29
  129.0 53.8 %all_to_all.66 = f32[8,1,65536]{2,1,0:T(1,128)} all-to-all(f32[8,1,65536]{2,1,0:T(1,128)} %reshape.172), channel_id=1, replica_groups=mesh['space'=8,'kern'=4] {'space'}, dimensions={0} | all-to-all | bytes 4194304 | tf_op jit(solution)/shard_map/all_to_all | solution.py:134
  183.3 8.5 %reduce = f32[8,65536]{1,0:T(8,128)} reduce(f32[8,1,65536]{2,1,0:T(1,128)} %all_to_all.66, f32[]{:T(128)} %broadcast.375), dimensions={1}, to_apply=%all_to_all.51.reduce_sub_computation | reduce | bytes 4194308 | tf_op jit(solution)/shard_map/all_to_all | solution.py:134
  209.2 16.7 %fusion.59 = f32[2,4,128,2048]{3,2,1,0:T(8,128)S(1)} fusion(f32[2,4,128,512]{3,2,1,0:T(8,128)} %bitcast.122, f32[512,1024]{1,0:T(8,128)} %get-tuple-element.573, f32[512,1024]{1,0:T(8,128)S(1)} %get-tuple-element.572), kind=kOutput, calls=%fused_computation.95 | convolution fusion | flops 12885950464 | bytes 14680064 | tf_op jit(solution)/shard_map/dot_general | solution.py:136
  230.2 32.4 %all-reduce.2.cloned.1.call-done = f32[128,1024]{1,0:T(8,128)} async-done(((f32[128,1024]{1,0:T(8,128)}), f32[128,1024]{1,0:T(8,128)}) %all-reduce.2.cloned.1.call-update) | async-done | bytes 524304 | tf_op jit(solution)/shard_map/psum | solution.py:146
  273.3 15.5 %fusion.54 = f32[512,2,4,128]{3,0,2,1:T(8,128)S(1)} fusion(f32[1,4,128,2048]{3,2,1,0:T(8,128)} %get-tuple-element.561, f32[1,4,128,2048]{3,2,1,0:T(8,128)} %get-tuple-element.560, f32[512,1024]{1,0:T(8,128)S(1)} %copy-done.3, f32[512,1024]{1,0:T(8,128)S(1)} %get-tuple-element.572), kind=kOutput, calls=%fused_computation.86 | convolution fusion | flops 12888047616 | bytes 14680064 | tf_op jit(solution)/shard_map/dot_general | solution.py:159
  290.1 53.1 %all_to_all.67 = f32[512,2,4,128]{3,2,1,0:T(4,128)S(1)} all-to-all(f32[512,2,4,128]{3,2,1,0:T(4,128)S(1)} %copy.63), channel_id=1, replica_groups=mesh['space'=8,'kern'=4] {'space'}, dimensions={0} | all-to-all | bytes 4194304 | tf_op jit(solution)/shard_map/all_to_all | solution.py:161
  361.6 8.9 %fusion.71 = f32[512,512]{1,0:T(8,128)S(1)} fusion(f32[512,2048]{1,0:T(8,128)} %reshape.168, f32[512,1024]{1,0:T(8,128)} %get-tuple-element.573, f32[512,1024]{1,0:T(8,128)S(1)} %get-tuple-element.572), kind=kOutput, calls=%fused_computation.117 | convolution fusion | flops 6443499520 | bytes 9437184 | tf_op jit(solution)/shard_map/dot_general | solution.py:171
  372.8 17.0 %reduce-scatter.3.cloned.1.call-done = f32[16,512]{1,0:T(8,128)} async-done(((f32[64,512]{1,0:T(8,128)}), f32[16,512]{1,0:T(8,128)}) %reduce-scatter.3.cloned.1.call-update) | async-done | bytes 32784 | tf_op jit(solution)/shard_map/reduce_scatter | solution.py:177
  390.5 21.9 %reduce-scatter.5.cloned.1.call-done = f32[16,512]{1,0:T(8,128)} async-done(((f32[64,512]{1,0:T(8,128)}), f32[16,512]{1,0:T(8,128)}) %reduce-scatter.5.cloned.1.call-update) | async-done | bytes 32784 | tf_op jit(solution)/shard_map/reduce_scatter | solution.py:178
  413.3 49.2 %while.64 = (s32[]{:T(128)}, f32[32,4096]{1,0:T(8,128)S(1)}, f32[32,1024]{1,0:T(8,128)S(1)}, s32[]{:T(128)}, s32[]{:T(128)}, /*index=5*/s32[]{:T(128)}, s32[]{:T(128)}) while((s32[]{:T(128)}, f32[32,4096]{1,0:T(8,128)S(1)}, f32[32,1024]{1,0:T(8,128)S(1)}, s32[]{:T(128)}, s32[]{:T(128)}, /*index=5*/s32[]{:T(128)}, ...), condition=%wide.region_11.12_spmd.clone, body=%wide.region_10.11_spmd.clone.sunk | while | flops 412616192 | bytes 8663171 | solution.py:85
  413.5 8.3 %fusion.107 = (f32[1024,512]{1,0:T(8,128)S(1)}, f32[1024,512]{1,0:T(8,128)S(1)}) fusion(s32[512]{0:T(512)S(1)} %iota_add_fusion.13, s32[1024]{0:T(1024)S(1)} %iota_add_fusion.14), kind=kLoop, calls=%fused_computation.20.clone.1 | loop fusion | flops 7864320 | bytes 4200448 | tf_op jit(solution)/shard_map/while/body/eval_jaxpr/cos | solution.py:29
  425.8 8.3 %fusion.107 = (f32[1024,512]{1,0:T(8,128)S(1)}, f32[1024,512]{1,0:T(8,128)S(1)}) fusion(s32[512]{0:T(512)S(1)} %iota_add_fusion.13, s32[1024]{0:T(1024)S(1)} %iota_add_fusion.14), kind=kLoop, calls=%fused_computation.20.clone.1 | loop fusion | flops 7864320 | bytes 4200448 | tf_op jit(solution)/shard_map/while/body/eval_jaxpr/cos | solution.py:29
  438.0 8.3 %fusion.107 = (f32[1024,512]{1,0:T(8,128)S(1)}, f32[1024,512]{1,0:T(8,128)S(1)}) fusion(s32[512]{0:T(512)S(1)} %iota_add_fusion.13, s32[1024]{0:T(1024)S(1)} %iota_add_fusion.14), kind=kLoop, calls=%fused_computation.20.clone.1 | loop fusion | flops 7864320 | bytes 4200448 | tf_op jit(solution)/shard_map/while/body/eval_jaxpr/cos | solution.py:29
  450.3 8.3 %fusion.107 = (f32[1024,512]{1,0:T(8,128)S(1)}, f32[1024,512]{1,0:T(8,128)S(1)}) fusion(s32[512]{0:T(512)S(1)} %iota_add_fusion.13, s32[1024]{0:T(1024)S(1)} %iota_add_fusion.14), kind=kLoop, calls=%fused_computation.20.clone.1 | loop fusion | flops 7864320 | bytes 4200448 | tf_op jit(solution)/shard_map/while/body/eval_jaxpr/cos | solution.py:29
  474.2 19.3 %all_to_all.68 = f32[8,1,16384]{2,1,0:T(1,128)S(1)} all-to-all(f32[8,1,16384]{2,1,0:T(1,128)S(1)} %reshape.174), channel_id=1, replica_groups=mesh['space'=8,'kern'=4] {'space'}, dimensions={0} | all-to-all | bytes 1048576 | tf_op jit(solution)/shard_map/all_to_all | solution.py:181
  509.4 20.8 %all-gather.2.cloned.1.call-done = f32[2,512,512]{2,1,0:T(8,128)} async-done(((f32[2,128,512]{2,1,0:T(8,128)}), f32[2,512,512]{2,1,0:T(8,128)}) %all-gather.2.cloned.1.call-update) | async-done | bytes 2097168 | tf_op jit(solution)/shard_map/all_gather | solution.py:188
  534.6 100.2 %while.65 = (s32[]{:T(128)}, f32[512,4096]{1,0:T(8,128)}, f32[1024,512]{1,0:T(8,128)}, s32[4,8]{1,0:T(4,128)S(1)}, s32[]{:T(128)}, /*index=5*/s32[]{:T(128)}, s32[]{:T(128)}, s32[]{:T(128)}) while((s32[]{:T(128)}, f32[512,4096]{1,0:T(8,128)}, f32[1024,512]{1,0:T(8,128)}, s32[4,8]{1,0:T(4,128)S(1)}, s32[]{:T(128)}, ...), condition=%wide.region_13.14_spmd.clone, body=%wide.region_12.13_spmd.clone.sunk | while | flops 6451890176 | bytes 39862572 | solution.py:99
  (161 shorter events, 282.1 us)
Async XLA Ops:
  30.4 21.7 %all-to-all-start = ((f32[2,128,512]{2,0,1:T(2,128)}), f32[2,128,512]{2,0,1:T(2,128)S(1)}, u32[]{:S(2)}, u32[]{:S(2)}) async-start(f32[2,128,512]{2,0,1:T(2,128)} %copy.57), calls=%async_computation | async-start | bytes 1048576 | tf_op jit(solution)/shard_map/all_to_all | solution.py:116
  37.6 225.0 %all-reduce.2.cloned.1.call-start = ((), (), s32[]{:S(2)}) async-start(), calls=%async_computation.6 | async-start | bytes 1048576 | tf_op jit(solution)/shard_map/psum | solution.py:146
  53.6 53.8 %copy-start.5 = (f32[2,4,64,512]{3,2,1,0:T(8,128)S(1)}, f32[2,4,64,512]{3,2,1,0:T(8,128)}, u32[]{:S(2)}) copy-start(f32[2,4,64,512]{3,2,1,0:T(8,128)} %param.12) | copy-start | bytes 3145732
  101.2 6.5 %copy-start.2 = (f32[512,1024]{1,0:T(8,128)S(1)}, f32[512,1024]{1,0:T(8,128)}, u32[]{:S(2)}) copy-start(f32[512,1024]{1,0:T(8,128)} %get-tuple-element.573) | copy-start | bytes 6291460
  225.9 3.4 copy-start
  230.2 159.6 %reduce-scatter.3.cloned.1.call-start = ((), (), s32[]{:S(2)}) async-start(), calls=%async_computation.7 | async-start | bytes 163840 | tf_op jit(solution)/shard_map/reduce_scatter | solution.py:177
  269.3 4.0 copy-start.3
  348.5 1.9 copy-start.4
  372.0 40.5 %reduce-scatter.5.cloned.1.call-start = ((), (), s32[]{:S(2)}) async-start(), calls=%async_computation.8 | async-start | bytes 163840 | tf_op jit(solution)/shard_map/reduce_scatter | solution.py:178
  372.7 157.5 %all-gather.2.cloned.1.call-start = ((), (), s32[]{:S(2)}) async-start(), calls=%async_computation.9 | async-start | bytes 2621440 | tf_op jit(solution)/shard_map/all_gather | solution.py:188
  540.1 8.3 %copy-start.1 = (f32[1024,512]{1,0:T(8,128)S(1)}, f32[1024,512]{1,0:T(8,128)}, u32[]{:S(2)}) copy-start(f32[1024,512]{1,0:T(8,128)} %get-tuple-element.762) | copy-start | bytes 6291460 | tf_op jit(solution)/shard_map/while
  565.1 8.3 %copy-start.1 = (f32[1024,512]{1,0:T(8,128)S(1)}, f32[1024,512]{1,0:T(8,128)}, u32[]{:S(2)}) copy-start(f32[1024,512]{1,0:T(8,128)} %get-tuple-element.762) | copy-start | bytes 6291460 | tf_op jit(solution)/shard_map/while
  590.1 8.3 %copy-start.1 = (f32[1024,512]{1,0:T(8,128)S(1)}, f32[1024,512]{1,0:T(8,128)}, u32[]{:S(2)}) copy-start(f32[1024,512]{1,0:T(8,128)} %get-tuple-element.762) | copy-start | bytes 6291460 | tf_op jit(solution)/shard_map/while
  615.1 8.3 %copy-start.1 = (f32[1024,512]{1,0:T(8,128)S(1)}, f32[1024,512]{1,0:T(8,128)}, u32[]{:S(2)}) copy-start(f32[1024,512]{1,0:T(8,128)} %get-tuple-element.762) | copy-start | bytes 6291460 | tf_op jit(solution)/shard_map/while
Sparse Core Ops, SparseCore 0:
  230.3 32.2 all-reduce.1
  372.1 17.5 reduce-scatter.2
  392.9 19.5 reduce-scatter.4
  509.4 20.7 all-gather.1
where the time goes:
time: 649 us; the launch traced here: 642 us
  other arithmetic  149 us (23%)
  blocking collectives  132 us (20%)
  matrix products  122 us (19%)
  local copies, waits for them, and re-layouts  118 us (18%)
  waiting for transfers between devices  97.6 us (15%)
  between operations  14.5 us (2%)
  starting transfers between devices  7.41 us (1%)
    cos x8, other arithmetic, row_table(): return jnp.concatenate([jnp.cos(angle), -jnp.sin(angle)], axis=1) / length  66.3 us
    all_to_all x1, blocking collectives, local(): lax.all_to_all(coarse, 'space', split_axis=3, concat_axis=0, tiled=True)  53.8 us
    all_to_all x1, blocking collectives, local(): lax.all_to_all(backward, 'space', split_axis=0, concat_axis=3, tiled=True)  53.1 us
    cos x8, other arithmetic, column_table(): return jnp.concatenate([jnp.cos(angle), -jnp.sin(angle)], axis=1)  41.7 us
    unnamed x15, local copies, waits for them, and re-layouts  33.1 us
    psum x1, waiting for transfers between devices, local(): intensity = lax.psum(partial_light, 'kern')  32.4 us
    dot_general x4, matrix products, step(): lax.dot_general(spectrum, table, (((0,), (1,)), ((), ())), precision=high...  32.1 us
    reduce_scatter x1, waiting for transfers between devices, local(): lax.psum_scatter(sum_im, 'kern', scatter_dimension=0, tiled=True)  21.9 us
  transfers between devices with their start and end apart: 5, of which 5 were waited for; matrix products, arithmetic and copies ran while one was open for 2% of the time, Pallas kernels for 0%

commit v1 on v0

--- a/solution.py
+++ b/solution.py
@@ -1,6 +1,12 @@
+import functools
+
 import jax
 import jax.numpy as jnp
+import ml_dtypes
+import numpy as np
 from jax import lax
+from jax.experimental import pallas as pl
+from jax.experimental.pallas import tpu as pltpu
 from jax.sharding import PartitionSpec as P
 
 N = 4096
@@ -191,7 +197,486 @@
     return (gradient, resist)
 
 
+MESH = pl.DeviceIdType.MESH
+
+
+def split_constant(values):
+    high = values.astype(np.float32).astype(ml_dtypes.bfloat16)
+    low = (values - high.astype(np.float64)).astype(ml_dtypes.bfloat16)
+    return jnp.asarray(high), jnp.asarray(low)
+
+
+def pixel_table(S, Q):
+    nx, P_ = S // Q, B // S
+    g = P_ // Q
+    y, z, x, i = np.meshgrid(np.arange(Q), np.arange(Q), np.arange(nx), np.arange(g), indexing="ij")
+    f = ((y * nx + x) * P_ + z * g + i - B // 2).reshape(-1, g)
+    angle = (f[:, :, None] * np.arange(N)) % N * (2 * np.pi / N)
+    table = np.stack([np.cos(angle), -np.sin(angle)], axis=1)
+    return jnp.asarray(table.reshape(2 * B, N).astype(np.float32))
+
+
+def coarse_tables(S):
+    f = np.arange(B) - B // 2
+    points = np.arange(G)
+    angle = (f[:, None] * points[None, :]) % G * (2 * np.pi / G)
+    c, s = np.cos(angle), np.sin(angle)
+    Y = G // S
+    cc = c.reshape(B, S, Y).transpose(1, 0, 2)
+    ss = s.reshape(B, S, Y).transpose(1, 0, 2)
+    lift = np.concatenate([np.concatenate([cc, ss], 2), np.concatenate([-ss, cc], 2)], 1)
+    forward = np.concatenate([c.T, s.T], 0)
+    backward = np.concatenate([c, s], 0)
+    return split_constant(lift) + split_constant(forward) + split_constant(backward)
+
+
+def halves(value):
+    high = value.astype(jnp.bfloat16)
+    return high, (value - high.astype(jnp.float32)).astype(jnp.bfloat16)
+
+
+def dot3(ah, al, bh, bl, dims):
+    d = functools.partial(lax.dot_general, dimension_numbers=(dims, ((), ())), preferred_element_type=jnp.float32)
+    return d(ah, bh) + (d(al, bh) + d(ah, bl))
+
+
+NN = ((1,), (0,))
+NT = ((1,), (1,))
+
+
+def remote(src, dst, send, recv, space, kern):
+    return pltpu.make_async_remote_copy(
+        src_ref=src, dst_ref=dst, send_sem=send, recv_sem=recv, device_id=(space, kern), device_id_type=MESH
+    )
+
+
+def scatter_kernel(S, R, x_ref, out_ref, send, recv, own):
+    sp, kq = lax.axis_index("space"), lax.axis_index("kern")
+    barrier = pltpu.get_barrier_semaphore()
+
+    def greet(o, c):
+        pl.semaphore_signal(barrier, inc=1, device_id=(lax.rem(sp + o, S), kq), device_id_type=MESH)
+        return c
+
+    lax.fori_loop(1, S, greet, 0)
+    pl.semaphore_wait(barrier, S - 1)
+    place = lambda s: out_ref.at[:, pl.ds(pl.multiple_of(s * R, R), R)]
+    local_copy = pltpu.make_async_copy(x_ref.at[sp], place(sp), own)
+    local_copy.start()
+
+    def launch(o, c):
+        d = lax.rem(sp + o, S)
+        remote(x_ref.at[d], place(sp), send.at[d], recv.at[sp], d, kq).start()
+        return c
+
+    lax.fori_loop(1, S, launch, 0)
+
+    def finish(o, c):
+        d = lax.rem(sp + o, S)
+        remote(x_ref.at[d], place(d), send.at[d], recv.at[d], d, kq).wait()
+        return c
+
+    lax.fori_loop(1, S, finish, 0)
+    local_copy.wait()
+
+
+def gather_kernel(S, Q, R, x_ref, out_ref, send, recv, ysend, yrecv, csend, crecv, own):
+    sp, kq = lax.axis_index("space"), lax.axis_index("kern")
+    kc = kq + 1 - 2 * lax.rem(kq, 2)
+    ky = lax.rem(kq + 2, Q)
+    kyc = lax.rem(kc + 2, Q)
+    barrier = pltpu.get_barrier_semaphore()
+
+    def greet(o, c):
+        pl.semaphore_signal(barrier, inc=1, device_id=(lax.rem(sp + o, S), kq), device_id_type=MESH)
+        return c
+
+    lax.fori_loop(1, S, greet, 0)
+    for k in (kc, ky):
+        pl.semaphore_signal(barrier, inc=1, device_id=(sp, k), device_id_type=MESH)
+    pl.semaphore_wait(barrier, S + 1)
+    slab = lambda s: x_ref.at[:, pl.ds(pl.multiple_of(s * R, R), R)]
+
+    def launch(o, c):
+        d = lax.rem(sp + o, S)
+        remote(slab(d), out_ref.at[kq, sp], send.at[d], recv.at[sp], d, kq).start()
+        return c
+
+    lax.fori_loop(1, S, launch, 0)
+    local_copy = pltpu.make_async_copy(slab(sp), out_ref.at[kq, sp], own)
+    local_copy.start()
+    local_copy.wait()
+
+    def to_y(s, group):
+        return remote(out_ref.at[group, s], out_ref.at[group, s], ysend.at[s], yrecv.at[s], sp, ky)
+
+    def to_core(s, group, slot):
+        return remote(out_ref.at[group, s], out_ref.at[group, s], csend.at[slot, s], crecv.at[slot, s], sp, kc)
+
+    to_y(sp, kq).start()
+    to_core(sp, kq, 0).start()
+
+    def onward(o, c):
+        s = lax.rem(sp + S - o, S)
+        remote(slab(s), out_ref.at[kq, s], send.at[s], recv.at[s], s, kq).wait_recv()
+        to_y(s, kq).start()
+        to_core(s, kq, 0).start()
+        return c
+
+    lax.fori_loop(1, S, onward, 0)
+
+    def across(o, c):
+        s = lax.rem(sp + S - o, S)
+        to_y(s, ky).wait_recv()
+        to_core(s, ky, 1).start()
+        return c
+
+    lax.fori_loop(0, S, across, 0)
+
+    def finish(s, c):
+        to_y(s, kq).wait_send()
+        to_core(s, kq, 0).wait_send()
+        to_core(s, ky, 1).wait_send()
+        to_core(s, kc, 0).wait_recv()
+        to_core(s, kyc, 1).wait_recv()
+        return c
+
+    lax.fori_loop(0, S, finish, 0)
+
+    def sent(o, c):
+        d = lax.rem(sp + o, S)
+        remote(slab(d), out_ref.at[kq, sp], send.at[d], recv.at[sp], d, kq).wait_send()
+        return c
+
+    lax.fori_loop(1, S, sent, 0)
+
+
+def imaging_kernel(
+    S, Q, K4,
+    spec_ref, kern_ref, target_ref, lh_hbm, ll_hbm, fh_hbm, fl_hbm, bh_hbm, bl_hbm,
+    out_ref, resist_ref,
+    lh, ll, fh, fl, bh, bl, table_sem,
+    specall, ph, pw, out1, in1, field, light, lightin, lightall, out2, in2, sums, rsin, acc,
+    spec_s, spec_r, s1, r1, ls, lr, as_, ar, s2, r2, rs, rr,
+):
+    nx, P_, Y = S // Q, B // S, G // S
+    g = P_ // Q
+    GQ = G // Q
+    sp, kq = lax.axis_index("space"), lax.axis_index("kern")
+    z, x = sp // nx, lax.rem(sp, nx)
+    blk = kq * nx + x
+    tables = [
+        pltpu.make_async_copy(src, dst, table_sem.at[i])
+        for i, (src, dst) in enumerate(
+            zip((lh_hbm, ll_hbm, fh_hbm, fl_hbm, bh_hbm, bl_hbm), (lh, ll, fh, fl, bh, bl))
+        )
+    ]
+    for t in tables:
+        t.start()
+
+    def member(o):
+        b = lax.rem(blk + o, S)
+        return b, z * nx + lax.rem(b, nx), b // nx
+
+    def zpeer(o):
+        q = lax.rem(z + o, Q)
+        return q, q * nx + x
+
+    barrier = pltpu.get_barrier_semaphore()
+
+    def greet(o, c):
+        b, s, k = member(o)
+        pl.semaphore_signal(barrier, inc=1, device_id=(s, k), device_id_type=MESH)
+        return c
+
+    lax.fori_loop(1, S, greet, 0)
+    for o in range(1, Q):
+        pl.semaphore_signal(barrier, inc=1, device_id=(zpeer(o)[1], kq), device_id_type=MESH)
+    pl.semaphore_wait(barrier, S + Q - 2)
+
+    def spec_copy(o, slot):
+        q, s = zpeer(o)
+        return remote(spec_ref, specall.at[slot], spec_s.at[q], spec_r.at[slot], s, kq)
+
+    for o in range(1, Q):
+        spec_copy(o, z).start()
+    specall[z] = spec_ref[...]
+    for o in range(1, Q):
+        spec_copy(o, zpeer(o)[0]).wait()
+
+    spec = specall[...].reshape(P_, 2 * B)
+    sr, si = spec[:, :B], spec[:, B:]
+    for k in range(K4):
+        kr, ki = kern_ref[0, k], kern_ref[1, k]
+        rows = pl.ds(k * P_, P_)
+        ph[rows, :B], pw[rows, :B] = halves(kr * sr - ki * si)
+        ph[rows, B:], pw[rows, B:] = halves(kr * si + ki * sr)
+
+    tables[0].wait()
+    tables[1].wait()
+    pair = K4 // 2
+
+    def copy1(k, b, s, kk, slot):
+        return remote(out1.at[k, b], in1.at[k, slot], s1.at[k, b], r1.at[k, slot], s, kk)
+
+    for h in range(2):
+        rows = pl.ds(h * pair * P_, pair * P_)
+        own = None
+
+        def lift(b):
+            return dot3(ph[rows, :], pw[rows, :], lh[b], ll[b], NN).reshape(pair, P_, 2 * Y)
+
+        def step(o, c):
+            b, s, kk = member(o)
+            value = lift(b)
+            for j in range(pair):
+                out1[h * pair + j, b] = value[j]
+            for j in range(pair):
+                copy1(h * pair + j, b, s, kk, blk).start()
+            return c
+
+        lax.fori_loop(1, S, step, 0)
+        value = lift(blk)
+        for j in range(pair):
+            in1[h * pair + j, blk] = value[j]
+
+    for t in tables[2:]:
+        t.wait()
+    chunk = 256
+
+    def image(k, c):
+        def arrive(o, c):
+            b, s, kk = member(o)
+            copy1(k, b, s, kk, b).wait_recv()
+            return c
+
+        lax.fori_loop(1, S, arrive, 0)
+        dh, dl = halves(in1[k].reshape(B, 2 * Y))
+
+        def part(j, c):
+            rows = pl.ds(pl.multiple_of(j * chunk, chunk), chunk)
+            low = pl.ds(pl.multiple_of(G + j * chunk, chunk), chunk)
+            a = dot3(fh[rows, :], fl[rows, :], dh, dl, NN)
+            b = dot3(fh[low, :], fl[low, :], dh, dl, NN)
+            re = a[:, :Y] - b[:, Y:]
+            im = a[:, Y:] + b[:, :Y]
+            field[k, rows, :Y] = re
+            field[k, rows, Y:] = im
+            power = re * re + im * im
+
+            @pl.when(k == 0)
+            def _():
+                light[rows, :] = power
+
+            @pl.when(k > 0)
+            def _():
+                light[rows, :] = light[rows, :] + power
+
+            return c
+
+        return lax.fori_loop(0, G // chunk, part, c)
+
+    lax.fori_loop(0, K4, image, 0)
+
+    quarter = lambda q: pl.ds(pl.multiple_of(q * GQ, GQ), GQ)
+
+    def light_copy(o, slot):
+        q, s = zpeer(o)
+        return remote(light.at[quarter(q)], lightin.at[slot], ls.at[q], lr.at[slot], s, kq)
+
+    for o in range(1, Q):
+        light_copy(o, z).start()
+    lightin[z] = light[quarter(z), :]
+    for o in range(1, Q):
+        light_copy(o, zpeer(o)[0]).wait()
+    total = lightin[0]
+    for q in range(1, Q):
+        total = total + lightin[q]
+    lightall[z] = total * (1.0 / (B * B))
+
+    def all_copy(o, slot):
+        q, s = zpeer(o)
+        return remote(lightall.at[z], lightall.at[slot], as_.at[q], ar.at[slot], s, kq)
+
+    for o in range(1, Q):
+        all_copy(o, z).start()
+    for o in range(1, Q):
+        all_copy(o, zpeer(o)[0]).wait_recv()
+    for q in range(Q):
+        rows = pl.ds(q * GQ, GQ)
+        resist = jax.nn.sigmoid(steepness * (lightall[q] - threshold))
+        resist_ref[rows, :] = resist
+        light[rows, :] = (4.0 * steepness / (B * B)) * (resist - target_ref[rows, :]) * resist * (1.0 - resist)
+
+    def copy2(k, b, s, kk, slot):
+        return remote(out2.at[k, b], in2.at[k, slot], s2.at[k, b], r2.at[k, slot], s, kk)
+
+    def back(k, c):
+        scale = light[...]
+        scale = jnp.concatenate([scale, scale], axis=1)
+        dh, dl = halves(field[k] * scale)
+
+        def part(j, c):
+            rows = pl.ds(pl.multiple_of(j * chunk, chunk), chunk)
+            low = pl.ds(pl.multiple_of(B + j * chunk, chunk), chunk)
+            a = dot3(bh[rows, :], bl[rows, :], dh, dl, NN)
+            b = dot3(bh[low, :], bl[low, :], dh, dl, NN)
+            value = jnp.concatenate([a[:, :Y] + b[:, Y:], a[:, Y:] - b[:, :Y]], axis=1)
+            out2[k, pl.ds(j * (chunk // P_), chunk // P_)] = value.reshape(chunk // P_, P_, 2 * Y)
+            return c
+
+        lax.fori_loop(0, B // chunk, part, c)
+
+        def launch(o, c):
+            b, s, kk = member(o)
+            copy2(k, b, s, kk, blk).start()
+            return c
+
+        lax.fori_loop(1, S, launch, 0)
+        in2[k, blk] = out2[k, blk]
+        return c
+
+    lax.fori_loop(0, K4, back, 0)
+
+    sum_re = jnp.zeros((P_, B), jnp.float32)
+    sum_im = jnp.zeros((P_, B), jnp.float32)
+    for h in range(2):
+        for j in range(pair):
+            def arrive2(o, c):
+                b, s, kk = member(o)
+                copy2(h * pair + j, b, s, kk, b).wait_recv()
+                return c
+
+            lax.fori_loop(1, S, arrive2, 0)
+        acc[...] = jnp.zeros_like(acc)
+
+        def add(s, c):
+            dh, dl = halves(in2[pl.ds(h * pair, pair), s].reshape(pair * P_, 2 * Y))
+            acc[...] += dot3(dh, dl, lh[s], ll[s], NT)
+            return c
+
+        lax.fori_loop(0, S, add, 0)
+        for j in range(pair):
+            k = h * pair + j
+            kr, ki = kern_ref[0, k], kern_ref[1, k]
+            pr, pi = acc[pl.ds(j * P_, P_), :B], acc[pl.ds(j * P_, P_), B:]
+            sum_re = sum_re + kr * pr + ki * pi
+            sum_im = sum_im + kr * pi - ki * pr
+    sums[:, :, :B] = sum_re.reshape(Q, g, B)
+    sums[:, :, B:] = sum_im.reshape(Q, g, B)
+
+    def sum_copy(o, slot):
+        q, s = zpeer(o)
+        return remote(sums.at[q], rsin.at[slot], rs.at[q], rr.at[slot], s, kq)
+
+    for o in range(1, Q):
+        sum_copy(o, z).start()
+    rsin[z] = sums[z]
+    for o in range(1, Q):
+        sum_copy(o, zpeer(o)[0]).wait()
+    total = rsin[0]
+    for q in range(1, Q):
+        total = total + rsin[q]
+    out_ref[...] = total
+
+    for o in range(1, Q):
+        all_copy(o, z).wait_send()
+
+    def drain(k, c):
+        def one(o, c):
+            b, s, kk = member(o)
+            copy1(k, b, s, kk, blk).wait_send()
+            copy2(k, b, s, kk, blk).wait_send()
+            return c
+
+        return lax.fori_loop(1, S, one, c)
+
+    lax.fori_loop(0, K4, drain, 0)
+
+
+def call(kernel, outs, specs, scratch, cid, args, mib):
+    vm = pl.BlockSpec(memory_space=pltpu.VMEM)
+    return pl.pallas_call(
+        kernel,
+        out_shape=outs,
+        in_specs=specs,
+        out_specs=jax.tree.map(lambda _: vm, outs),
+        scratch_shapes=scratch,
+        compiler_params=pltpu.CompilerParams(
+            collective_id=cid, has_side_effects=True, vmem_limit_bytes=mib * 2**20
+        ),
+    )(*args)
+
+
+def fast(S, Q, mask, kernels, target):
+    f32, bf16 = jnp.float32, jnp.bfloat16
+    nx, P_, Y, R = S // Q, B // S, G // S, N // S
+    g, K4 = P_ // Q, kernels.shape[1]
+    DMA = pltpu.SemaphoreType.DMA
+    vm, any_ = pl.BlockSpec(memory_space=pltpu.VMEM), pl.BlockSpec(memory_space=pl.ANY)
+    high = lax.Precision.HIGH
+    kq = lax.axis_index("kern")
+    table = pixel_table(S, Q)
+    swap = [
+        (((zz * nx) + xx) * Q + kk, ((kk * nx) + xx) * Q + zz)
+        for zz in range(Q) for xx in range(nx) for kk in range(Q)
+    ]
+    kern_here = lax.ppermute(kernels, ("space", "kern"), swap)
+    target_here = lax.ppermute(target, ("space", "kern"), swap).T.astype(f32)
+
+    rows = lax.dynamic_slice_in_dim(table, kq * (2 * B // Q), 2 * B // Q, 0)
+    columns = lax.dot_general(rows, mask.astype(f32), (((1,), (1,)), ((), ())), precision=high)
+    arrived = call(
+        functools.partial(scatter_kernel, S, R),
+        jax.ShapeDtypeStruct((2 * g, N), f32), [vm],
+        [DMA((S,)), DMA((S,)), DMA],
+        0, (columns.reshape(S, 2 * g, R),), 16,
+    )
+    t = lax.dot_general(arrived, table, (((1,), (1,)), ((), ())), precision=high) * (1.0 / N)
+    t = t.reshape(2, g, Q, Q, nx, 2, g).transpose(0, 1, 5, 2, 4, 3, 6).reshape(2, g, 2, B)
+    spec = jnp.concatenate([t[0, :, 0] - t[1, :, 1], t[0, :, 1] + t[1, :, 0]], axis=1)
+
+    consts = coarse_tables(S)
+    V = pltpu.VMEM
+    total, resist = call(
+        functools.partial(imaging_kernel, S, Q, K4),
+        (jax.ShapeDtypeStruct((g, 2 * B), f32), jax.ShapeDtypeStruct((G, Y), f32)),
+        [vm, vm, vm] + [any_] * 6,
+        [V(c.shape, bf16) for c in consts] + [DMA((6,))] + [
+            V((Q, g, 2 * B), f32),
+            V((K4 * P_, 2 * B), bf16), V((K4 * P_, 2 * B), bf16),
+            V((K4, S, P_, 2 * Y), f32), V((K4, S, P_, 2 * Y), f32),
+            V((K4, G, 2 * Y), f32), V((G, Y), f32),
+            V((Q, G // Q, Y), f32), V((Q, G // Q, Y), f32),
+            V((K4, S, P_, 2 * Y), f32), V((K4, S, P_, 2 * Y), f32),
+            V((Q, g, 2 * B), f32), V((Q, g, 2 * B), f32),
+            V((K4 // 2 * P_, 2 * B), f32),
+            DMA((Q,)), DMA((Q,)), DMA((K4, S)), DMA((K4, S)),
+            DMA((Q,)), DMA((Q,)), DMA((Q,)), DMA((Q,)),
+            DMA((K4, S)), DMA((K4, S)), DMA((Q,)), DMA((Q,)),
+        ],
+        1, (spec, kern_here, target_here) + consts, 56,
+    )
+    resist = lax.ppermute(resist, ("space", "kern"), swap).T
+
+    re, im = total[:, :B], total[:, B:]
+    stacked = jnp.stack([jnp.stack([re, im], 1), jnp.stack([im, -re], 1)])
+    stacked = stacked.reshape(2, g, 2, Q, nx, Q, g).transpose(0, 1, 3, 5, 4, 2, 6).reshape(2 * g, 2 * B)
+    delta = jnp.dot(stacked, table, precision=high) * (1.0 / N)
+    piece = call(
+        functools.partial(gather_kernel, S, Q, R),
+        jax.ShapeDtypeStruct((Q, S, 2 * g, R), f32), [vm],
+        [DMA((S,)), DMA((S,)), DMA((S,)), DMA((S,)), DMA((2, S)), DMA((2, S)), DMA],
+        2, (delta,), 16,
+    )
+    gradient = lax.dot_general(piece.reshape(2 * B, R), table, (((0,), (0,)), ((), ())), precision=high)
+    return gradient, resist
+
+
 def solution(mesh):
     in_specs = (P("space", None), P(None, "kern", "space", None), P("space", None))
     out_specs = (P("space", None), P("space", None))
-    return jax.shard_map(local, mesh=mesh, in_specs=in_specs, out_specs=out_specs, check_vma=False)
+    S, Q = mesh.shape["space"], mesh.shape["kern"]
+    whole_tiles = Q == 4 and S % Q == 0 and (B // S // Q) % 16 == 0 and (G // S) % 128 == 0
+    body = functools.partial(fast, S, Q) if whole_tiles else local
+    return jax.shard_map(body, mesh=mesh, in_specs=in_specs, out_specs=out_specs, check_vma=False)

time: 649 us -> 293 us (0.45)
  Pallas kernels: 0 us -> 223 us
  other arithmetic: 149 us -> 4.37 us
  blocking collectives: 132 us -> 0 us
  local copies, waits for them, and re-layouts: 118 us -> 9.63 us
  waiting for transfers between devices: 97.6 us -> 0.01 us
  matrix products: 122 us -> 45.3 us
  between operations: 14.5 us -> 0.78 us
    pallas_call x0 -> x3, Pallas kernels: none -> 223 us  [call(): pl.pallas_call(kernel, out_shape=outs, in_specs=specs, out_specs=jax.tree...]
    all_to_all x3 -> x0, blocking collectives: 126 us -> none  [the longest x1 53.8 us: local(): lax.all_to_all(coarse, 'space', split_axis=3, concat_axis=0, tiled=True)]
    cos x17 -> x0, other arithmetic: 118 us -> none  [the longest x8 66.3 us: row_table(): return jnp.concatenate([jnp.cos(angle), -jnp.sin(angle)], axis=1) / length]
    dot_general x20 -> x4, matrix products: 122 us -> 45.3 us  [the longest x1 20 us: fast(): lax.dot_general(piece.reshape(2 * B, R), table, (((0,), (0,)), ((), ())),...]
    reduce_scatter x2 -> x0, waiting for transfers between devices: 38.9 us -> none  [the longest x1 21.9 us: local(): lax.psum_scatter(sum_im, 'kern', scatter_dimension=0, tiled=True)]
    psum x1 -> x0, waiting for transfers between devices: 32.4 us -> none  [local(): intensity = lax.psum(partial_light, 'kern')]
    unnamed x15 -> x6, local copies, waits for them, and re-layouts: 33.1 us -> 4.01 us
    all_gather x1 -> x0, waiting for transfers between devices: 20.8 us -> none  [local(): piece = lax.all_gather(landed, 'kern', axis=1, tiled=True)]
  transfers between devices with their start and end apart: 5 -> 3, of which waited for: 5 -> 0; matrix products, arithmetic and copies ran while one was open for 2% -> 14% of each run, Pallas kernels for 0% -> 40%
where the time goes in v1:
time: 293 us; the launch traced here: 291 us
  Pallas kernels  223 us (76%)
  matrix products  45.3 us (15%)
  local copies, waits for them, and re-layouts  9.63 us (3%)
  starting transfers between devices  7.92 us (3%)
  other arithmetic  4.37 us (1%)
    pallas_call x3, Pallas kernels, call(): pl.pallas_call(kernel, out_shape=outs, in_specs=specs, out_specs=jax.tree...  223 us
    dot_general x1, matrix products, fast(): lax.dot_general(piece.reshape(2 * B, R), table, (((0,), (0,)), ((), ())),...  20 us
    dot_general x1, matrix products, fast(): lax.dot_general(arrived, table, (((1,), (1,)), ((), ())), precision=high)  10.9 us
    dot_general x1, matrix products, fast(): delta = jnp.dot(stacked, table, precision=high) * (1.0 / N)  8.65 us
  transfers between devices with their start and end apart: 3, of which 0 were waited for; matrix products, arithmetic and copies ran while one was open for 14% of the time, Pallas kernels for 40%

profile of v1, /device:TPU:0, one launch (start us, length us, event | category | flops | bytes accessed | tf_op | source)
XLA Modules:
  0.0 290.7 jit_solution(4594142681878809199)
XLA Ops:
  0.6 2.0 copy.16
  2.7 5.3 %collective-permute-start.1 = (s32[128,1024]{0,1:T(8,128)}, s32[128,1024]{0,1:T(8,128)}, u32[]{:S(2)}, u32[]{:S(2)}) collective-permute-start(s32[128,1024]{0,1:T(8,128)} %copy.16), channel_id=1, source_target_pairs={{0,0},{1,8},{2,16},{3,24},{4,4},{5,12},{6,20},{7,28},{8,1},{9,9},{... | collective-permute-start | bytes 1572872 | tf_op jit(solution)/shard_map/ppermute | solution.py:625
  8.0 1.9 collective-permute-start
  9.9 5.8 %fusion = f32[256,512]{1,0:T(8,128)S(1)} fusion(bf16[512,4096]{1,0:T(8,128)(2,1)} %param.10, f32[1024,4096]{1,0:T(8,128)} %constant.11.clone, s32[]{:T(128)S(6)} %select_n.3), kind=kOutput, calls=%fused_computation.1 | convolution fusion | flops 3221225472 | bytes 8912900 | tf_op jit(solution)/shard_map/dot_general | solution.py:628
  15.7 71.3 %shard_map.113 = f32[32,4096]{1,0:T(8,128)S(1)} custom-call(f32[8,32,512]{2,1,0:T(8,128)S(1)} %bitcast.24), custom_call_target="tpu_custom_call" | custom-call | tf_op jit(solution)/shard_map/pallas_call | solution.py:599
  87.0 10.9 %convolution_multiply_fusion.1 = f32[32,1024]{1,0:T(8,128)S(1)} fusion(f32[32,4096]{1,0:T(8,128)S(1)} %shard_map.113, f32[1024,4096]{1,0:T(8,128)} %constant.11.clone), kind=kOutput, calls=%fused_computation.3 | convolution fusion | flops 805339136 | bytes 17432576 | tf_op jit(solution)/shard_map/dot_general | solution.py:635
  97.9 1.4 reshape.35
  99.3 0.3 copy.23
  99.6 0.9 reshape.36
  100.6 0.6 pad_maximum_fusion.spec_ref
  101.2 1.9 convert_bitcast_fusion.target_ref
  103.1 1.0 copy-done
  104.1 105.7 %shard_map.114 = (f32[16,1024]{1,0:T(8,128)}, f32[1024,128]{1,0:T(8,128)}) custom-call(f32[16,1024]{1,0:T(8,128)} %pad_maximum_fusion.spec_ref, f32[2,4,64,512]{3,2,1,0:T(8,128)} %copy-done, f32[1024,128]{1,0:T(8,128)} %convert_bitcast_fusion.target_ref, bf16[8,1024,256]{2,1,0:T(8,128)(2,1)} %constant.28.clone.lh_hbm, ...), custom_call_target="tpu_custom_call" | custom-call | tf_op jit(solution)/shard_map/pallas_call | solution.py:599
  209.8 0.8 fusion.5
  210.8 0.3 copy.17
  211.3 0.3 copy.20
  211.8 0.3 copy.18
  212.1 1.1 maximum_bitcast_fusion
  213.2 1.5 reshape.37
  214.7 8.6 %convolution_multiply_fusion.x_ref = f32[32,4096]{1,0:T(8,128)S(1)} fusion(f32[32,1024]{1,0:T(8,128)S(1)} %reshape.37, f32[1024,4096]{1,0:T(8,128)} %constant.11.clone), kind=kOutput, calls=%fused_computation | convolution fusion | flops 805437440 | bytes 17432576 | tf_op jit(solution)/shard_map/dot_general | solution.py:665
  223.4 0.7 collective-permute-start.2
  224.1 45.6 %shard_map.115 = f32[4,8,32,512]{3,2,1,0:T(8,128)S(1)} custom-call(f32[32,4096]{1,0:T(8,128)S(1)} %convolution_multiply_fusion.x_ref), custom_call_target="tpu_custom_call" | custom-call | tf_op jit(solution)/shard_map/pallas_call | solution.py:599
  269.7 20.0 %fusion.6 = f32[512,4096]{1,0:T(8,128)} fusion(f32[1024,512]{1,0:T(8,128)S(1)} %bitcast.23, f32[1024,4096]{1,0:T(8,128)} %constant.11.clone), kind=kOutput, calls=%fused_computation.15 | convolution fusion | flops 12884901888 | bytes 27262976 | tf_op jit(solution)/shard_map/dot_general | solution.py:672
  289.7 1.0 copy.21
  (10 shorter events, 0.7 us)
Async XLA Ops:
  2.7 98.5 %collective-permute-start.1 = (s32[128,1024]{0,1:T(8,128)}, s32[128,1024]{0,1:T(8,128)}, u32[]{:S(2)}, u32[]{:S(2)}) collective-permute-start(s32[128,1024]{0,1:T(8,128)} %copy.16), channel_id=1, source_target_pairs={{0,0},{1,8},{2,16},{3,24},{4,4},{5,12},{6,20},{7,28},{8,1},{9,9},{... | collective-permute-start | bytes 1572872 | tf_op jit(solution)/shard_map/ppermute | solution.py:625
  8.0 95.1 %collective-permute-start = (f32[2,4,64,512]{3,2,1,0:T(8,128)}, f32[2,4,64,512]{3,2,1,0:T(8,128)S(1)}, u32[]{:S(2)}, u32[]{:S(2)}) collective-permute-start(f32[2,4,64,512]{3,2,1,0:T(8,128)} %param.11), channel_id=1, source_target_pairs={{0,0},{1,8},{2,16},{3,24},{4,4},{5,12},{6,20},{7,28},{8,1},{9,9},{... | collective-permute-start | bytes 3145736 | tf_op jit(solution)/shard_map/ppermute | solution.py:624
  103.1 1.0 copy-start
  214.7 8.7 %copy-start.1 = (f32[1024,128]{1,0:T(8,128)S(1)}, f32[1024,128]{1,0:T(8,128)}, u32[]{:S(2)}) copy-start(f32[1024,128]{1,0:T(8,128)} %get-tuple-element.5) | copy-start | bytes 1572868
  223.4 66.3 %collective-permute-start.2 = (f32[1024,128]{1,0:T(8,128)S(1)}, f32[1024,128]{1,0:T(8,128)S(1)}, u32[]{:S(2)}, u32[]{:S(2)}) collective-permute-start(f32[1024,128]{1,0:T(8,128)S(1)} %copy-done.1), channel_id=1, source_target_pairs={{0,0},{1,8},{2,16},{3,24},{4,4},{5,12},{6,20},{7,28},{8,1},{9,9},{... | collective-permute-start | bytes 1572872 | tf_op jit(solution)/shard_map/ppermute | solution.py:660

commit v2 on v1

--- a/solution.py
+++ b/solution.py
@@ -206,14 +206,10 @@
     return jnp.asarray(high), jnp.asarray(low)
 
 
-def pixel_table(S, Q):
-    nx, P_ = S // Q, B // S
-    g = P_ // Q
-    y, z, x, i = np.meshgrid(np.arange(Q), np.arange(Q), np.arange(nx), np.arange(g), indexing="ij")
-    f = ((y * nx + x) * P_ + z * g + i - B // 2).reshape(-1, g)
-    angle = (f[:, :, None] * np.arange(N)) % N * (2 * np.pi / N)
-    table = np.stack([np.cos(angle), -np.sin(angle)], axis=1)
-    return jnp.asarray(table.reshape(2 * B, N).astype(np.float32))
+def pixel_table():
+    f = np.arange(B) - B // 2
+    angle = (f[:, None] * np.arange(N)) % N * (2 * np.pi / N)
+    return jnp.asarray(np.concatenate([np.cos(angle), -np.sin(angle)]).astype(np.float32))
 
 
 def coarse_tables(S):
@@ -250,113 +246,14 @@
     )
 
 
-def scatter_kernel(S, R, x_ref, out_ref, send, recv, own):
-    sp, kq = lax.axis_index("space"), lax.axis_index("kern")
-    barrier = pltpu.get_barrier_semaphore()
-
-    def greet(o, c):
-        pl.semaphore_signal(barrier, inc=1, device_id=(lax.rem(sp + o, S), kq), device_id_type=MESH)
-        return c
-
-    lax.fori_loop(1, S, greet, 0)
-    pl.semaphore_wait(barrier, S - 1)
-    place = lambda s: out_ref.at[:, pl.ds(pl.multiple_of(s * R, R), R)]
-    local_copy = pltpu.make_async_copy(x_ref.at[sp], place(sp), own)
-    local_copy.start()
-
-    def launch(o, c):
-        d = lax.rem(sp + o, S)
-        remote(x_ref.at[d], place(sp), send.at[d], recv.at[sp], d, kq).start()
-        return c
-
-    lax.fori_loop(1, S, launch, 0)
-
-    def finish(o, c):
-        d = lax.rem(sp + o, S)
-        remote(x_ref.at[d], place(d), send.at[d], recv.at[d], d, kq).wait()
-        return c
-
-    lax.fori_loop(1, S, finish, 0)
-    local_copy.wait()
-
-
-def gather_kernel(S, Q, R, x_ref, out_ref, send, recv, ysend, yrecv, csend, crecv, own):
-    sp, kq = lax.axis_index("space"), lax.axis_index("kern")
-    kc = kq + 1 - 2 * lax.rem(kq, 2)
-    ky = lax.rem(kq + 2, Q)
-    kyc = lax.rem(kc + 2, Q)
-    barrier = pltpu.get_barrier_semaphore()
-
-    def greet(o, c):
-        pl.semaphore_signal(barrier, inc=1, device_id=(lax.rem(sp + o, S), kq), device_id_type=MESH)
-        return c
-
-    lax.fori_loop(1, S, greet, 0)
-    for k in (kc, ky):
-        pl.semaphore_signal(barrier, inc=1, device_id=(sp, k), device_id_type=MESH)
-    pl.semaphore_wait(barrier, S + 1)
-    slab = lambda s: x_ref.at[:, pl.ds(pl.multiple_of(s * R, R), R)]
-
-    def launch(o, c):
-        d = lax.rem(sp + o, S)
-        remote(slab(d), out_ref.at[kq, sp], send.at[d], recv.at[sp], d, kq).start()
-        return c
-
-    lax.fori_loop(1, S, launch, 0)
-    local_copy = pltpu.make_async_copy(slab(sp), out_ref.at[kq, sp], own)
-    local_copy.start()
-    local_copy.wait()
-
-    def to_y(s, group):
-        return remote(out_ref.at[group, s], out_ref.at[group, s], ysend.at[s], yrecv.at[s], sp, ky)
-
-    def to_core(s, group, slot):
-        return remote(out_ref.at[group, s], out_ref.at[group, s], csend.at[slot, s], crecv.at[slot, s], sp, kc)
-
-    to_y(sp, kq).start()
-    to_core(sp, kq, 0).start()
-
-    def onward(o, c):
-        s = lax.rem(sp + S - o, S)
-        remote(slab(s), out_ref.at[kq, s], send.at[s], recv.at[s], s, kq).wait_recv()
-        to_y(s, kq).start()
-        to_core(s, kq, 0).start()
-        return c
-
-    lax.fori_loop(1, S, onward, 0)
-
-    def across(o, c):
-        s = lax.rem(sp + S - o, S)
-        to_y(s, ky).wait_recv()
-        to_core(s, ky, 1).start()
-        return c
-
-    lax.fori_loop(0, S, across, 0)
-
-    def finish(s, c):
-        to_y(s, kq).wait_send()
-        to_core(s, kq, 0).wait_send()
-        to_core(s, ky, 1).wait_send()
-        to_core(s, kc, 0).wait_recv()
-        to_core(s, kyc, 1).wait_recv()
-        return c
-
-    lax.fori_loop(0, S, finish, 0)
-
-    def sent(o, c):
-        d = lax.rem(sp + o, S)
-        remote(slab(d), out_ref.at[kq, sp], send.at[d], recv.at[sp], d, kq).wait_send()
-        return c
-
-    lax.fori_loop(1, S, sent, 0)
-
-
 def imaging_kernel(
     S, Q, K4,
-    spec_ref, kern_ref, target_ref, lh_hbm, ll_hbm, fh_hbm, fl_hbm, bh_hbm, bl_hbm,
+    part_ref, kern_mine, target_mine, lh_hbm, ll_hbm, fh_hbm, fl_hbm, bh_hbm, bl_hbm,
     out_ref, resist_ref,
     lh, ll, fh, fl, bh, bl, table_sem,
+    kern_ref, target_ref, rbuf, specin, specq,
     specall, ph, pw, out1, in1, field, light, lightin, lightall, out2, in2, sums, rsin, acc,
+    ps, pr_, ks, kr_, ts, tr, us, ur, gs, gr, cs, cr, zs, zr,
     spec_s, spec_r, s1, r1, ls, lr, as_, ar, s2, r2, rs, rr,
 ):
     nx, P_, Y = S // Q, B // S, G // S
@@ -383,35 +280,74 @@
         return q, q * nx + x
 
     barrier = pltpu.get_barrier_semaphore()
+    swapped = z != kq
 
     def greet(o, c):
-        b, s, k = member(o)
-        pl.semaphore_signal(barrier, inc=1, device_id=(s, k), device_id_type=MESH)
+        pl.semaphore_signal(barrier, inc=1, device_id=(lax.rem(sp + o, S), kq), device_id_type=MESH)
         return c
 
     lax.fori_loop(1, S, greet, 0)
-    for o in range(1, Q):
-        pl.semaphore_signal(barrier, inc=1, device_id=(zpeer(o)[1], kq), device_id_type=MESH)
-    pl.semaphore_wait(barrier, S + Q - 2)
+    for dk in range(1, Q):
+        for xx in range(nx):
+            pl.semaphore_signal(
+                barrier, inc=1, device_id=(z * nx + xx, lax.rem(kq + dk, Q)), device_id_type=MESH
+            )
+
+    @pl.when(swapped)
+    def _():
+        pl.semaphore_signal(barrier, inc=1, device_id=(kq * nx + x, z), device_id_type=MESH)
+
+    pl.semaphore_wait(barrier, S - 1 + (Q - 1) * nx + jnp.where(swapped, 1, 0))
+
+    def part_copy(d, slot):
+        return remote(part_ref.at[lax.rem(d, nx), d // nx], specin.at[slot], ps.at[d], pr_.at[slot], d, kq)
+
+    def part_start(o, c):
+        part_copy(lax.rem(sp + o, S), sp).start()
+        return c
+
+    lax.fori_loop(1, S, part_start, 0)
+    specin[sp] = part_ref[x, z]
+
+    def kern_copy(k):
+        return remote(kern_mine.at[:, k], kern_ref.at[:, k], ks.at[k], kr_.at[k], kq * nx + x, z)
+
+    target_copy = remote(target_mine, target_ref, ts, tr, kq * nx + x, z)
+
+    @pl.when(swapped)
+    def _():
+        for k in range(K4):
+            kern_copy(k).start()
+        target_copy.start()
+
+    @pl.when(jnp.logical_not(swapped))
+    def _():
+        kern_ref[...] = kern_mine[...]
+        target_ref[...] = target_mine[...]
+
+    def part_wait(o, c):
+        d = lax.rem(sp + o, S)
+        part_copy(d, d).wait()
+        return c
+
+    lax.fori_loop(1, S, part_wait, 0)
+    total = specin[0]
+    for d in range(1, S):
+        total = total + specin[d]
+    specq[...] = total
 
     def spec_copy(o, slot):
         q, s = zpeer(o)
-        return remote(spec_ref, specall.at[slot], spec_s.at[q], spec_r.at[slot], s, kq)
+        return remote(specq, specall.at[slot], spec_s.at[q], spec_r.at[slot], s, kq)
 
     for o in range(1, Q):
         spec_copy(o, z).start()
-    specall[z] = spec_ref[...]
+    specall[z] = total
     for o in range(1, Q):
         spec_copy(o, zpeer(o)[0]).wait()
 
     spec = specall[...].reshape(P_, 2 * B)
     sr, si = spec[:, :B], spec[:, B:]
-    for k in range(K4):
-        kr, ki = kern_ref[0, k], kern_ref[1, k]
-        rows = pl.ds(k * P_, P_)
-        ph[rows, :B], pw[rows, :B] = halves(kr * sr - ki * si)
-        ph[rows, B:], pw[rows, B:] = halves(kr * si + ki * sr)
-
     tables[0].wait()
     tables[1].wait()
     pair = K4 // 2
@@ -420,8 +356,17 @@
         return remote(out1.at[k, b], in1.at[k, slot], s1.at[k, b], r1.at[k, slot], s, kk)
 
     for h in range(2):
+        @pl.when(swapped)
+        def _():
+            for j in range(pair):
+                kern_copy(h * pair + j).wait()
+
+        for k in range(h * pair, h * pair + pair):
+            kr, ki = kern_ref[0, k], kern_ref[1, k]
+            rows = pl.ds(k * P_, P_)
+            ph[rows, :B], pw[rows, :B] = halves(kr * sr - ki * si)
+            ph[rows, B:], pw[rows, B:] = halves(kr * si + ki * sr)
         rows = pl.ds(h * pair * P_, pair * P_)
-        own = None
 
         def lift(b):
             return dot3(ph[rows, :], pw[rows, :], lh[b], ll[b], NN).reshape(pair, P_, 2 * Y)
@@ -502,11 +447,26 @@
         all_copy(o, z).start()
     for o in range(1, Q):
         all_copy(o, zpeer(o)[0]).wait_recv()
+
+    @pl.when(swapped)
+    def _():
+        target_copy.wait()
+
     for q in range(Q):
         rows = pl.ds(q * GQ, GQ)
         resist = jax.nn.sigmoid(steepness * (lightall[q] - threshold))
-        resist_ref[rows, :] = resist
+        rbuf[rows, :] = resist
         light[rows, :] = (4.0 * steepness / (B * B)) * (resist - target_ref[rows, :]) * resist * (1.0 - resist)
+
+    resist_copy = remote(rbuf, resist_ref, us, ur, kq * nx + x, z)
+
+    @pl.when(swapped)
+    def _():
+        resist_copy.start()
+
+    @pl.when(jnp.logical_not(swapped))
+    def _():
+        resist_ref[...] = rbuf[...]
 
     def copy2(k, b, s, kk, slot):
         return remote(out2.at[k, b], in2.at[k, slot], s2.at[k, b], r2.at[k, slot], s, kk)
@@ -577,7 +537,59 @@
     total = rsin[0]
     for q in range(1, Q):
         total = total + rsin[q]
-    out_ref[...] = total
+    out_ref[blk, z] = total
+
+    def z_copy(o, slot):
+        q, s = zpeer(o)
+        return remote(out_ref.at[blk, z], out_ref.at[blk, slot], zs.at[q], zr.at[slot], s, kq)
+
+    def z_from(o):
+        q, s = zpeer(o)
+        return remote(out_ref.at[blk, q], out_ref.at[blk, q], zs.at[q], zr.at[q], s, kq)
+
+    for o in range(1, Q):
+        z_copy(o, z).start()
+    for o in range(1, Q):
+        z_from(o).wait_recv()
+    kc = kq + 1 - 2 * lax.rem(kq, 2)
+    others = []
+    for dx in range(nx):
+        for dy in range(2):
+            if dx or dy:
+                kk, xx = lax.rem(kq + 2 * dy, Q), lax.rem(x + dx, nx)
+                xf = lax.rem(x + nx - dx, nx)
+                others.append((kk, xx, kk * nx + xx, xf, kk * nx + xf))
+
+    def to_core(b):
+        return remote(out_ref.at[b], out_ref.at[b], cs.at[b], cr.at[b], sp, kc)
+
+    def to_brick(other):
+        kk, xx, b, xf, bf = other
+        return remote(out_ref.at[blk], out_ref.at[blk], gs.at[b], gr.at[blk], z * nx + xx, kk)
+
+    def from_brick(other):
+        kk, xx, b, xf, bf = other
+        return remote(out_ref.at[bf], out_ref.at[bf], gs.at[b], gr.at[bf], z * nx + xf, kk)
+
+    for other in others:
+        to_brick(other).start()
+    to_core(blk).start()
+    for other in others:
+        from_brick(other).wait_recv()
+        to_core(other[4]).start()
+    for kk, xx in [(kq, x)] + [(o[0], o[3]) for o in others]:
+        mine = kk * nx + xx
+        theirs = (kk + 1 - 2 * lax.rem(kk, 2)) * nx + xx
+        to_core(mine).wait_send()
+        to_core(theirs).wait_recv()
+    for other in others:
+        to_brick(other).wait_send()
+    for o in range(1, Q):
+        z_copy(o, z).wait_send()
+
+    @pl.when(swapped)
+    def _():
+        resist_copy.wait()
 
     for o in range(1, Q):
         all_copy(o, z).wait_send()
@@ -615,34 +627,25 @@
     DMA = pltpu.SemaphoreType.DMA
     vm, any_ = pl.BlockSpec(memory_space=pltpu.VMEM), pl.BlockSpec(memory_space=pl.ANY)
     high = lax.Precision.HIGH
-    kq = lax.axis_index("kern")
-    table = pixel_table(S, Q)
-    swap = [
-        (((zz * nx) + xx) * Q + kk, ((kk * nx) + xx) * Q + zz)
-        for zz in range(Q) for xx in range(nx) for kk in range(Q)
-    ]
-    kern_here = lax.ppermute(kernels, ("space", "kern"), swap)
-    target_here = lax.ppermute(target, ("space", "kern"), swap).T.astype(f32)
-
-    rows = lax.dynamic_slice_in_dim(table, kq * (2 * B // Q), 2 * B // Q, 0)
+    sp, kq = lax.axis_index("space"), lax.axis_index("kern")
+    table = pixel_table()
+    C = B // Q
+
+    rows = jnp.concatenate([lax.dynamic_slice_in_dim(table, part * B + kq * C, C, 0) for part in range(2)], axis=0)
     columns = lax.dot_general(rows, mask.astype(f32), (((1,), (1,)), ((), ())), precision=high)
-    arrived = call(
-        functools.partial(scatter_kernel, S, R),
-        jax.ShapeDtypeStruct((2 * g, N), f32), [vm],
-        [DMA((S,)), DMA((S,)), DMA],
-        0, (columns.reshape(S, 2 * g, R),), 16,
-    )
-    t = lax.dot_general(arrived, table, (((1,), (1,)), ((), ())), precision=high) * (1.0 / N)
-    t = t.reshape(2, g, Q, Q, nx, 2, g).transpose(0, 1, 5, 2, 4, 3, 6).reshape(2, g, 2, B)
-    spec = jnp.concatenate([t[0, :, 0] - t[1, :, 1], t[0, :, 1] + t[1, :, 0]], axis=1)
+    slab = lax.dynamic_slice_in_dim(table, sp * R, R, 1) * (1.0 / N)
+    t = lax.dot_general(columns, slab, (((1,), (1,)), ((), ())), precision=high)
+    part = jnp.concatenate([t[:C, :B] - t[C:, B:], t[:C, B:] + t[C:, :B]], axis=1)
 
     consts = coarse_tables(S)
     V = pltpu.VMEM
     total, resist = call(
         functools.partial(imaging_kernel, S, Q, K4),
-        (jax.ShapeDtypeStruct((g, 2 * B), f32), jax.ShapeDtypeStruct((G, Y), f32)),
+        (jax.ShapeDtypeStruct((S, Q, g, 2 * B), f32), jax.ShapeDtypeStruct((G, Y), f32)),
         [vm, vm, vm] + [any_] * 6,
         [V(c.shape, bf16) for c in consts] + [DMA((6,))] + [
+            V((2, K4, P_, B), f32), V((G, Y), f32), V((G, Y), f32),
+            V((S, g, 2 * B), f32), V((g, 2 * B), f32),
             V((Q, g, 2 * B), f32),
             V((K4 * P_, 2 * B), bf16), V((K4 * P_, 2 * B), bf16),
             V((K4, S, P_, 2 * Y), f32), V((K4, S, P_, 2 * Y), f32),
@@ -651,26 +654,23 @@
             V((K4, S, P_, 2 * Y), f32), V((K4, S, P_, 2 * Y), f32),
             V((Q, g, 2 * B), f32), V((Q, g, 2 * B), f32),
             V((K4 // 2 * P_, 2 * B), f32),
+            DMA((S,)), DMA((S,)), DMA((K4,)), DMA((K4,)), DMA, DMA, DMA, DMA,
+            DMA((S,)), DMA((S,)), DMA((S,)), DMA((S,)), DMA((Q,)), DMA((Q,)),
             DMA((Q,)), DMA((Q,)), DMA((K4, S)), DMA((K4, S)),
             DMA((Q,)), DMA((Q,)), DMA((Q,)), DMA((Q,)),
             DMA((K4, S)), DMA((K4, S)), DMA((Q,)), DMA((Q,)),
         ],
-        1, (spec, kern_here, target_here) + consts, 56,
-    )
-    resist = lax.ppermute(resist, ("space", "kern"), swap).T
-
-    re, im = total[:, :B], total[:, B:]
-    stacked = jnp.stack([jnp.stack([re, im], 1), jnp.stack([im, -re], 1)])
-    stacked = stacked.reshape(2, g, 2, Q, nx, Q, g).transpose(0, 1, 3, 5, 4, 2, 6).reshape(2 * g, 2 * B)
-    delta = jnp.dot(stacked, table, precision=high) * (1.0 / N)
-    piece = call(
-        functools.partial(gather_kernel, S, Q, R),
-        jax.ShapeDtypeStruct((Q, S, 2 * g, R), f32), [vm],
-        [DMA((S,)), DMA((S,)), DMA((S,)), DMA((S,)), DMA((2, S)), DMA((2, S)), DMA],
-        2, (delta,), 16,
-    )
-    gradient = lax.dot_general(piece.reshape(2 * B, R), table, (((0,), (0,)), ((), ())), precision=high)
-    return gradient, resist
+        1, (part.reshape(nx, Q, g, 2 * B), kernels, target.T.astype(f32)) + consts, 58,
+    )
+
+    total = total.reshape(B, 2 * B)
+    a, b = slab[:B], slab[B:]
+    delta = jnp.concatenate([
+        jnp.dot(total, slab, precision=high),
+        jnp.dot(total, jnp.concatenate([-b, a], axis=0), precision=high),
+    ], axis=0)
+    gradient = lax.dot_general(lax.optimization_barrier(delta), table, (((0,), (0,)), ((), ())), precision=high)
+    return gradient, resist.T
 
 
 def solution(mesh):

time: 293 us -> 265 us (0.904)
  matrix products: 45.3 us -> 31.8 us
  starting transfers between devices: 7.92 us -> 0 us
  local copies, waits for them, and re-layouts: 9.63 us -> 6.52 us
  Pallas kernels: 223 us -> 220 us
    dot_general x3 -> x4, matrix products: 39.5 us -> 29.5 us  [the longest x1 19.6 us: fast(): lax.dot_general(lax.optimization_barrier(delta), table, (((0,), (0,)), ((...]
    ppermute x3 -> x0, starting transfers between devices: 7.92 us -> none  [the longest x1 5.35 us: fast(): target_here = lax.ppermute(target, ('space', 'kern'), swap).T.astype(f32)]
    reshape x4 -> x0, local copies, waits for them, and re-layouts: 4.15 us -> none  [the longest x3 2.61 us: fast(): t.reshape(2, g, Q, Q, nx, 2, g).transpose(0, 1, 5, 2, 4, 3, 6)]
    dot_general x1, matrix products: 5.82 us -> 2.36 us  [fast(): lax.dot_general(rows, mask.astype(f32), (((1,), (1,)), ((), ())), precisi...]
    pallas_call x3 -> x1, Pallas kernels: 223 us -> 220 us  [call(): pl.pallas_call(kernel, out_shape=outs, in_specs=specs, out_specs=jax.tree...]
  transfers between devices with their start and end apart: 3 -> 0, of which waited for: 0 -> 0; matrix products, arithmetic and copies ran while one was open for 14% -> 0% of each run, Pallas kernels for 40% -> 0%
where the time goes in v2:
time: 265 us; the launch traced here: 263 us
  Pallas kernels  220 us (83%)
  matrix products  31.8 us (12%)
  local copies, waits for them, and re-layouts  6.52 us (2%)
  other arithmetic  3.94 us (1%)
    pallas_call x1, Pallas kernels, call(): pl.pallas_call(kernel, out_shape=outs, in_specs=specs, out_specs=jax.tree...  220 us
    dot_general x1, matrix products, fast(): lax.dot_general(lax.optimization_barrier(delta), table, (((0,), (0,)), ((...  19.6 us

profile of v2, /device:TPU:0, one launch (start us, length us, event | category | flops | bytes accessed | tf_op | source)
XLA Modules:
  0.0 262.6 jit_solution(12676423096008720898)
XLA Ops:
  0.6 1.2 copy.12
  1.9 0.8 convert_bitcast_fusion.target_mine
  2.7 1.8 dynamic-slice_multiply_fusion
  4.5 0.2 slice_negate_fusion
  4.8 0.0 copy-start.1
  4.8 2.7 %constant_dynamic-slice_fusion.1 = (f32[128,4096]{1,0:T(8,128)S(1)}, f32[128,4096]{1,0:T(8,128)S(1)}) fusion(f32[1024,4096]{1,0:T(8,128)} %constant.37.clone, s32[]{:T(128)S(6)} %select_n.9, s32[]{:T(128)S(6)} %select_n.10), kind=kLoop, calls=%fused_computation.22 | loop fusion | bytes 8388616 | tf_op jit(solution)/shard_map/dynamic_slice | solution.py:634
  7.4 0.8 copy-done.1
  8.2 2.4 fusion
  10.6 2.7 %fusion.9 = f32[256,1024]{1,0:T(8,128)S(1)} fusion(f32[256,512]{1,0:T(8,128)S(1)} %fusion, f32[1024,4096]{1,0:T(8,128)} %constant.37.clone, s32[]{:T(128)S(6)} %select_n.11), kind=kOutput, calls=%fused_computation.11 | convolution fusion | flops 805830656 | bytes 3670020 | tf_op jit(solution)/shard_map/dot_general | solution.py:637
  13.3 0.1 slice_subtract_fusion
  13.4 0.8 pad_maximum_fusion.1
  14.2 219.6 %shard_map.113 = (f32[8,4,16,1024]{3,2,1,0:T(8,128)}, f32[1024,128]{1,0:T(8,128)}) custom-call(f32[2,4,16,1024]{3,2,1,0:T(8,128)} %bitcast.13, f32[2,4,64,512]{3,2,1,0:T(8,128)} %kern_mine.1, f32[1024,128]{1,0:T(8,128)} %convert_bitcast_fusion.target_mine, bf16[8,1024,256]{2,1,0:T(8,128)(2,1)} %constant.38.clone.lh_hbm, ...), custom_call_target="tpu_custom_call" | custom-call | tf_op jit(solution)/shard_map/pallas_call | solution.py:611
  233.8 0.0 copy-start
  233.8 3.6 %fusion.4 = f32[512,512]{1,0:T(8,128)S(1)} fusion(f32[512,1024]{1,0:T(8,128)} %bitcast.11, f32[512,512]{1,0:T(8,128)S(1)} %get-tuple-element.11, f32[512,512]{1,0:T(8,128)S(1)} %get-tuple-element.10), kind=kOutput, calls=%fused_computation.4 | convolution fusion | flops 1611137024 | bytes 5242880 | tf_op jit(solution)/shard_map/dot_general | solution.py:670
  237.4 0.0 copy-done
  237.4 3.5 %fusion.8 = f32[512,512]{1,0:T(8,128)S(1)} fusion(f32[512,1024]{1,0:T(8,128)S(1)} %bitcast.12, f32[1024,4096]{1,0:T(8,128)} %constant.37.clone, s32[]{:T(128)S(6)} %select_n.11), kind=kOutput, calls=%fused_computation.10 | convolution fusion | flops 1611137024 | bytes 5242884 | tf_op jit(solution)/shard_map/dot_general | solution.py:669
  241.0 0.0 copy-start.2
  241.0 0.2 pad_maximum_fusion
  241.2 0.9 copy-done.2
  242.0 1.0 copy.13
  243.0 19.6 %fusion.18 = f32[512,4096]{1,0:T(8,128)} fusion(f32[1024,512]{1,0:T(8,128)S(1)} %pad_maximum_fusion, f32[1024,4096]{1,0:T(8,128)} %constant.37.clone), kind=kOutput, calls=%fused_computation.27 | convolution fusion | flops 12884901888 | bytes 27262976 | tf_op jit(solution)/shard_map/dot_general | solution.py:672
Async XLA Ops:
  4.8 3.5 %copy-start.1 = (bf16[512,4096]{1,0:T(8,128)(2,1)S(1)}, bf16[512,4096]{1,0:T(8,128)(2,1)}, u32[]{:S(2)}) copy-start(bf16[512,4096]{1,0:T(8,128)(2,1)} %param.10) | copy-start | bytes 12582916
  233.8 3.6 %copy-start = (f32[8,4,16,1024]{3,2,1,0:T(8,128)S(1)}, f32[8,4,16,1024]{3,2,1,0:T(8,128)}, u32[]{:S(2)}) copy-start(f32[8,4,16,1024]{3,2,1,0:T(8,128)} %get-tuple-element.4) | copy-start | bytes 6291460
  241.0 1.0 copy-start.2

commit v3 on v2

--- a/solution.py
+++ b/solution.py
@@ -246,6 +246,10 @@
     )
 
 
+def crossed(v):
+    return 2 * lax.rem(v, 2) + v // 2
+
+
 def imaging_kernel(
     S, Q, K4,
     part_ref, kern_mine, target_mine, lh_hbm, ll_hbm, fh_hbm, fl_hbm, bh_hbm, bl_hbm,
@@ -261,7 +265,7 @@
     GQ = G // Q
     sp, kq = lax.axis_index("space"), lax.axis_index("kern")
     z, x = sp // nx, lax.rem(sp, nx)
-    blk = kq * nx + x
+    blk = crossed(kq) * nx + x
     tables = [
         pltpu.make_async_copy(src, dst, table_sem.at[i])
         for i, (src, dst) in enumerate(
@@ -273,14 +277,15 @@
 
     def member(o):
         b = lax.rem(blk + o, S)
-        return b, z * nx + lax.rem(b, nx), b // nx
+        return b, z * nx + lax.rem(b, nx), crossed(b // nx)
 
     def zpeer(o):
         q = lax.rem(z + o, Q)
         return q, q * nx + x
 
     barrier = pltpu.get_barrier_semaphore()
-    swapped = z != kq
+    swapped = z != crossed(kq)
+    partner = (crossed(kq) * nx + x, crossed(z))
 
     def greet(o, c):
         pl.semaphore_signal(barrier, inc=1, device_id=(lax.rem(sp + o, S), kq), device_id_type=MESH)
@@ -295,7 +300,7 @@
 
     @pl.when(swapped)
     def _():
-        pl.semaphore_signal(barrier, inc=1, device_id=(kq * nx + x, z), device_id_type=MESH)
+        pl.semaphore_signal(barrier, inc=1, device_id=partner, device_id_type=MESH)
 
     pl.semaphore_wait(barrier, S - 1 + (Q - 1) * nx + jnp.where(swapped, 1, 0))
 
@@ -310,9 +315,9 @@
     specin[sp] = part_ref[x, z]
 
     def kern_copy(k):
-        return remote(kern_mine.at[:, k], kern_ref.at[:, k], ks.at[k], kr_.at[k], kq * nx + x, z)
-
-    target_copy = remote(target_mine, target_ref, ts, tr, kq * nx + x, z)
+        return remote(kern_mine.at[:, k], kern_ref.at[:, k], ks.at[k], kr_.at[k], *partner)
+
+    target_copy = remote(target_mine, target_ref, ts, tr, *partner)
 
     @pl.when(swapped)
     def _():
@@ -458,7 +463,7 @@
         rbuf[rows, :] = resist
         light[rows, :] = (4.0 * steepness / (B * B)) * (resist - target_ref[rows, :]) * resist * (1.0 - resist)
 
-    resist_copy = remote(rbuf, resist_ref, us, ur, kq * nx + x, z)
+    resist_copy = remote(rbuf, resist_ref, us, ur, *partner)
 
     @pl.when(swapped)
     def _():
@@ -558,7 +563,7 @@
             if dx or dy:
                 kk, xx = lax.rem(kq + 2 * dy, Q), lax.rem(x + dx, nx)
                 xf = lax.rem(x + nx - dx, nx)
-                others.append((kk, xx, kk * nx + xx, xf, kk * nx + xf))
+                others.append((kk, xx, crossed(kk) * nx + xx, xf, crossed(kk) * nx + xf))
 
     def to_core(b):
         return remote(out_ref.at[b], out_ref.at[b], cs.at[b], cr.at[b], sp, kc)
@@ -578,8 +583,8 @@
         from_brick(other).wait_recv()
         to_core(other[4]).start()
     for kk, xx in [(kq, x)] + [(o[0], o[3]) for o in others]:
-        mine = kk * nx + xx
-        theirs = (kk + 1 - 2 * lax.rem(kk, 2)) * nx + xx
+        mine = crossed(kk) * nx + xx
+        theirs = crossed(kk + 1 - 2 * lax.rem(kk, 2)) * nx + xx
         to_core(mine).wait_send()
         to_core(theirs).wait_recv()
     for other in others:
@@ -631,7 +636,7 @@
     table = pixel_table()
     C = B // Q
 
-    rows = jnp.concatenate([lax.dynamic_slice_in_dim(table, part * B + kq * C, C, 0) for part in range(2)], axis=0)
+    rows = jnp.concatenate([lax.dynamic_slice_in_dim(table, part * B + crossed(kq) * C, C, 0) for part in range(2)], axis=0)
     columns = lax.dot_general(rows, mask.astype(f32), (((1,), (1,)), ((), ())), precision=high)
     slab = lax.dynamic_slice_in_dim(table, sp * R, R, 1) * (1.0 / N)
     t = lax.dot_general(columns, slab, (((1,), (1,)), ((), ())), precision=high)

time: 265 us -> 232 us (0.88)
  Pallas kernels: 220 us -> 189 us
    pallas_call x1, Pallas kernels: 220 us -> 189 us  [call(): pl.pallas_call(kernel, out_shape=outs, in_specs=specs, out_specs=jax.tree...]
where the time goes in v3:
time: 232 us
  Pallas kernels  189 us (81%)
  matrix products  31.8 us (14%)
  local copies, waits for them, and re-layouts  6.52 us (3%)
  other arithmetic  3.94 us (2%)
    pallas_call x1, Pallas kernels, call(): pl.pallas_call(kernel, out_shape=outs, in_specs=specs, out_specs=jax.tree...  189 us
    dot_general x1, matrix products, fast(): lax.dot_general(lax.optimization_barrier(delta), table, (((0,), (0,)), ((...  19.6 us

profile of v3, /device:TPU:0, one launch (start us, length us, event | category | flops | bytes accessed | tf_op | source)
XLA Modules:
  0.0 231.6 jit_solution(1767275368692424936)
XLA Ops:
  0.7 1.2 copy.12
  1.9 0.8 convert_bitcast_fusion.target_mine
  2.7 1.8 dynamic-slice_multiply_fusion
  4.6 0.2 slice_negate_fusion
  4.8 0.0 copy-start.1
  4.8 2.7 %constant_dynamic-slice_fusion.1 = (f32[128,4096]{1,0:T(8,128)S(1)}, f32[128,4096]{1,0:T(8,128)S(1)}) fusion(f32[1024,4096]{1,0:T(8,128)} %constant.53.clone, s32[]{:T(128)S(6)} %select_n.16, s32[]{:T(128)S(6)} %select_n.17), kind=kLoop, calls=%fused_computation.22 | loop fusion | bytes 8388616 | tf_op jit(solution)/shard_map/dynamic_slice | solution.py:639
  7.5 0.8 copy-done.1
  8.2 2.4 %fusion = f32[256,512]{1,0:T(8,128)S(1)} fusion(bf16[512,4096]{1,0:T(8,128)(2,1)S(1)} %copy-done.1, f32[128,4096]{1,0:T(8,128)S(1)} %get-tuple-element.9, f32[128,4096]{1,0:T(8,128)S(1)} %get-tuple-element.8), kind=kOutput, calls=%fused_computation | convolution fusion | flops 3222274048 | bytes 8912896 | tf_op jit(solution)/shard_map/dot_general | solution.py:640
  10.6 2.7 %fusion.9 = f32[256,1024]{1,0:T(8,128)S(1)} fusion(f32[256,512]{1,0:T(8,128)S(1)} %fusion, f32[1024,4096]{1,0:T(8,128)} %constant.53.clone, s32[]{:T(128)S(6)} %select_n.18), kind=kOutput, calls=%fused_computation.11 | convolution fusion | flops 805830656 | bytes 3670020 | tf_op jit(solution)/shard_map/dot_general | solution.py:642
  13.3 0.1 slice_subtract_fusion
  13.4 0.8 pad_maximum_fusion.1
  14.2 188.5 %shard_map.113 = (f32[8,4,16,1024]{3,2,1,0:T(8,128)}, f32[1024,128]{1,0:T(8,128)}) custom-call(f32[2,4,16,1024]{3,2,1,0:T(8,128)} %bitcast.13, f32[2,4,64,512]{3,2,1,0:T(8,128)} %kern_mine.1, f32[1024,128]{1,0:T(8,128)} %convert_bitcast_fusion.target_mine, bf16[8,1024,256]{2,1,0:T(8,128)(2,1)} %constant.54.clone.lh_hbm, ...), custom_call_target="tpu_custom_call" | custom-call | tf_op jit(solution)/shard_map/pallas_call | solution.py:616
  202.8 0.0 copy-start
  202.8 3.6 %fusion.4 = f32[512,512]{1,0:T(8,128)S(1)} fusion(f32[512,1024]{1,0:T(8,128)} %bitcast.11, f32[512,512]{1,0:T(8,128)S(1)} %get-tuple-element.11, f32[512,512]{1,0:T(8,128)S(1)} %get-tuple-element.10), kind=kOutput, calls=%fused_computation.4 | convolution fusion | flops 1611137024 | bytes 5242880 | tf_op jit(solution)/shard_map/dot_general | solution.py:675
  206.4 0.0 copy-done
  206.4 3.5 %fusion.8 = f32[512,512]{1,0:T(8,128)S(1)} fusion(f32[512,1024]{1,0:T(8,128)S(1)} %bitcast.12, f32[1024,4096]{1,0:T(8,128)} %constant.53.clone, s32[]{:T(128)S(6)} %select_n.18), kind=kOutput, calls=%fused_computation.10 | convolution fusion | flops 1611137024 | bytes 5242884 | tf_op jit(solution)/shard_map/dot_general | solution.py:674
  209.9 0.0 copy-start.2
  210.0 0.2 pad_maximum_fusion
  210.1 0.9 copy-done.2
  211.0 1.0 copy.13
  212.0 19.6 %fusion.18 = f32[512,4096]{1,0:T(8,128)} fusion(f32[1024,512]{1,0:T(8,128)S(1)} %pad_maximum_fusion, f32[1024,4096]{1,0:T(8,128)} %constant.53.clone), kind=kOutput, calls=%fused_computation.27 | convolution fusion | flops 12884901888 | bytes 27262976 | tf_op jit(solution)/shard_map/dot_general | solution.py:677
Async XLA Ops:
  4.8 3.5 %copy-start.1 = (bf16[512,4096]{1,0:T(8,128)(2,1)S(1)}, bf16[512,4096]{1,0:T(8,128)(2,1)}, u32[]{:S(2)}) copy-start(bf16[512,4096]{1,0:T(8,128)(2,1)} %param.10) | copy-start | bytes 12582916
  202.8 3.6 %copy-start = (f32[8,4,16,1024]{3,2,1,0:T(8,128)S(1)}, f32[8,4,16,1024]{3,2,1,0:T(8,128)}, u32[]{:S(2)}) copy-start(f32[8,4,16,1024]{3,2,1,0:T(8,128)} %get-tuple-element.4) | copy-start | bytes 6291460
  209.9 1.0 copy-start.2
